TPU v7x, 128 devices: a whole 4x4x4 slice. The times are simulated.
128 devices in a mesh: rows: 32 (over z, y, core), cols: 4 (over x).
Axes of the slice: x: 4, y: 4, z: 4, core: 2. Of those that a mesh axis runs over, the one named last changes fastest.
Arguments:
- basis: float32 [64, 262144], P('cols', 'rows'), may hold values from -450 to 450
- blocks: bfloat16 [1024, 4, 256, 256], P('rows'), may hold values from -16 to 1, as said below
- far_cols: int32 [1024], P('rows'), may hold values from 0 to 1023, as said below
Outputs:
- basis_out: float32 [64, 262144], P('cols', 'rows')
- ritz: float32 [64, 64], P(None, 'cols')
Inputs may be any that keep to these rules, and one draw needn't show every extreme that they name: Off-diagonal entries are positive; each diagonal entry of a diagonal block is minus the sum of the other entries of its row over the four blocks, rounded to bfloat16. `far_cols`: the block rows of one device name at most 2 far columns among the block rows of any one device; the block rows of some device are named by exactly 2 block rows of every device.
All inputs are finite; a program needn't handle non-finite values.
Results may differ from a plain program's by a relative error of at most 0.0036.
Values may be sent and summed in bfloat16 or wider, within the bound.
No kernel may reach another device: no remote copies, remote signals or barrier semaphores. Data moves between devices by JAX's collectives and lax.ppermute only.
A program may use at most 128 MiB of HBM per device.

v0:
```python
import jax
import jax.numpy as jnp
from jax import lax
from jax.sharding import PartitionSpec as P

ITERS = 4


def with_halo(block, sides, width):
    for axis, dim in sides:
        count = lax.axis_size(axis)
        forward = [(i, i + 1) for i in range(count - 1)]
        forward.append((count - 1, 0))
        backward = [(target, source) for source, target in forward]
        low = lax.ppermute(
            lax.slice_in_dim(block, block.shape[dim] - width, None, axis=dim), axis, forward
        )
        high = lax.ppermute(lax.slice_in_dim(block, 0, width, axis=dim), axis, backward)
        block = jnp.concatenate([low, block, high], axis=dim)
    return block


def block_product(pieces, blocks, position):
    return jnp.einsum(
        "jbt,bst->jbs", pieces, blocks[:, position], preferred_element_type=jnp.float32
    )


def body(basis, blocks, far_cols):
    width = basis.shape[0]
    block_rows = blocks.shape[0]
    block_size = blocks.shape[2]
    row_devices = lax.axis_size("rows")
    total_states = block_rows * block_size * row_devices
    modes = width * lax.axis_size("cols")
    highest = lax.Precision.HIGHEST

    def apply_generator(iterate_bf):
        shaped = iterate_bf.reshape(width, block_rows, block_size)
        result = block_product(shaped, blocks, 0)
        empty = jnp.zeros((width, block_rows, block_size), jnp.bfloat16)
        piece = lax.all_gather(shaped, "rows", axis=1, tiled=True)
        inside = jnp.logical_and(far_cols >= 0, far_cols < piece.shape[1])
        taken = jnp.take(piece, jnp.clip(far_cols, 0, piece.shape[1] - 1), axis=1)
        remote = jnp.where(inside[None, :, None], taken, empty)
        extended = with_halo(shaped, (("rows", 1),), 1)
        result = result + block_product(extended[:, :-2], blocks, 1)
        result = result + block_product(extended[:, 2:], blocks, 2)
        result = result + block_product(remote, blocks, 3)
        return result.reshape(width, block_rows * block_size)

    iterate = basis
    for step in range(ITERS):
        iterate = iterate + 0.2 * apply_generator(iterate.astype(jnp.bfloat16))
    whole_iterate = lax.all_gather(iterate, "cols", axis=0, tiled=True)
    contract = (((1,), (1,)), ((), ()))
    gram_part = lax.dot_general(whole_iterate, iterate, contract, precision=highest)
    column_start = lax.axis_index("cols") * width
    gram_mine = lax.psum(gram_part, "rows")
    gram = lax.all_gather(gram_mine, "cols", axis=1, tiled=True) / total_states
    applied = apply_generator(iterate.astype(jnp.bfloat16))
    product_part = lax.dot_general(whole_iterate, applied, contract, precision=highest)
    product_mine = lax.psum(product_part, "rows")
    product = lax.all_gather(product_mine, "cols", axis=1, tiled=True) / total_states
    factor = jnp.linalg.cholesky(gram)
    identity_square = jnp.eye(modes, dtype=factor.dtype)
    inverse_factor = lax.linalg.triangular_solve(
        factor, identity_square, left_side=True, lower=True
    )
    own_rows = lax.dynamic_slice_in_dim(inverse_factor, column_start, width, 0)
    basis_out = jnp.dot(own_rows, whole_iterate, precision=highest)
    left_part = jnp.dot(inverse_factor, product, precision=highest)
    ritz_whole = jnp.dot(left_part, inverse_factor.T, precision=highest)
    ritz = lax.dynamic_slice_in_dim(ritz_whole, column_start, width, 1)
    return (basis_out, ritz)


def solution(mesh):
    in_specs = (P("cols", "rows"), P("rows", None, None, None), P("rows"))
    out_specs = (P("cols", "rows"), P(None, "cols"))
    return jax.shard_map(body, mesh=mesh, in_specs=in_specs, out_specs=out_specs, check_vma=False)
```

profile of v0, /device:TPU:0, one launch (start us, length us, event | category | flops | bytes accessed | tf_op | source)
XLA Modules:
  0.0 539.1 jit_solution(13265493274930220181)
XLA Ops:
  7.2 1.1 convert_element_type.16
  8.3 0.7 copy.158
  9.1 0.7 fusion.238
  9.8 6.0 %collective-permute-start.1 = (bf16[16,1,256]{2,0,1:T(8,128)(2,1)S(1)}, bf16[16,1,256]{2,0,1:T(8,128)(2,1)S(1)}, u32[]{:S(2)}, u32[]{:S(2)}) collective-permute-start(bf16[16,1,256]{2,0,1:T(8,128)(2,1)S(1)} %get-tuple-element.23), channel_id=1, source_target_pairs={{4,0},{8,4},{12,8},{16,12},{20,16},{24,20},{28,24},{32,28},{36,32}... | collective-permute-start | bytes 24584 | tf_op jit(solution)/shard_map/ppermute | solution.py:18
  15.8 0.7 compare_and_fusion
  16.5 3.4 fusion.60
  19.9 3.6 fusion.84
  23.5 3.5 fusion.81
  27.0 39.3 %all-gather.7.cloned.1.call-done = bf16[16,1024,256]{2,0,1:T(8,128)(2,1)} async-done(((bf16[16,32,256]{2,0,1:T(8,128)(2,1)}), bf16[16,1024,256]{2,0,1:T(8,128)(2,1)}) %all-gather.7.cloned.1.call-update) | async-done | bytes 8388624 | tf_op jit(solution)/shard_map/all_gather | solution.py:42
  66.4 3.9 gather_fusion
  70.3 3.4 fusion.72
  73.9 0.7 copy.157
  74.7 0.7 fusion.237
  75.4 2.8 collective-permute-start.3
  78.2 3.4 fusion.36
  81.6 3.6 fusion.16
  85.2 42.1 %all-gather.9.cloned.1.call-done = bf16[16,1024,256]{2,0,1:T(8,128)(2,1)} async-done(((bf16[16,32,256]{2,0,1:T(8,128)(2,1)}), bf16[16,1024,256]{2,0,1:T(8,128)(2,1)}) %all-gather.9.cloned.1.call-update) | async-done | bytes 8388624 | tf_op jit(solution)/shard_map/all_gather | solution.py:42
  127.3 3.9 gather_fusion.1
  131.2 3.4 fusion.6
  134.7 3.4 fusion.141
  138.2 0.7 copy.156
  139.0 0.7 fusion.236
  139.7 2.8 collective-permute-start.5
  142.5 3.4 fusion.34
  145.9 3.6 fusion.14
  149.6 42.1 %all-gather.11.cloned.1.call-done = bf16[16,1024,256]{2,0,1:T(8,128)(2,1)} async-done(((bf16[16,32,256]{2,0,1:T(8,128)(2,1)}), bf16[16,1024,256]{2,0,1:T(8,128)(2,1)}) %all-gather.11.cloned.1.call-update) | async-done | bytes 8388624 | tf_op jit(solution)/shard_map/all_gather | solution.py:42
  191.6 3.9 gather_fusion.2
  195.6 3.4 fusion.4
  199.0 3.4 fusion.129
  202.5 0.7 copy.155
  203.3 0.7 fusion.235
  204.0 2.8 collective-permute-start.7
  206.9 3.4 fusion.32
  210.3 3.6 fusion.12
  213.9 42.1 %all-gather.13.cloned.1.call-done = bf16[16,1024,256]{2,0,1:T(8,128)(2,1)} async-done(((bf16[16,32,256]{2,0,1:T(8,128)(2,1)}), bf16[16,1024,256]{2,0,1:T(8,128)(2,1)}) %all-gather.13.cloned.1.call-update) | async-done | bytes 8388624 | tf_op jit(solution)/shard_map/all_gather | solution.py:42
  256.0 3.9 gather_fusion.3
  259.9 3.4 fusion.2
  263.3 3.4 fusion.117
  266.8 0.9 fusion.230
  267.7 0.7 copy.154
  268.5 0.7 fusion.234
  269.2 2.8 collective-permute-start.9
  272.0 3.4 fusion.30
  275.5 3.8 fusion.10
  279.3 18.8 %all-gather.15.cloned.1.call-done = f32[64,8192]{1,0:T(8,128)} async-done(((f32[16,8192]{1,0:T(8,128)}), f32[64,8192]{1,0:T(8,128)}) %all-gather.15.cloned.1.call-update) | async-done | bytes 2097168 | tf_op jit(solution)/shard_map/all_gather | solution.py:55
  298.1 3.3 fusion.239
  301.5 51.9 %all-gather.17.cloned.1.call-done = bf16[16,1024,256]{2,0,1:T(8,128)(2,1)} async-done(((bf16[16,32,256]{2,0,1:T(8,128)(2,1)}), bf16[16,1024,256]{2,0,1:T(8,128)(2,1)}) %all-gather.17.cloned.1.call-update) | async-done | bytes 8388624 | tf_op jit(solution)/shard_map/all_gather | solution.py:42
  353.3 3.9 gather_fusion.4
  357.3 3.4 fusion
  360.7 3.6 fusion.105
  364.4 1.7 fusion.240
  366.1 126.6 %all-reduce = (f32[64,16]{0,1:T(8,128)S(1)}, f32[64,16]{0,1:T(8,128)S(1)}) all-reduce(f32[64,16]{0,1:T(8,128)S(1)} %fusion.239, f32[64,16]{0,1:T(8,128)S(1)} %fusion.240), channel_id=1, replica_groups=mesh['rows'=32,'cols'=4] {'rows'}, use_global_device_ids=true, to_apply=%region_0.2 | all-reduce | flops 2048 | bytes 16384 | tf_op jit(solution)/shard_map/psum | solution.py:59
  492.6 12.4 %all_gather.29 = f32[64,64]{0,1:T(8,128)S(1)} all-gather(f32[64,16]{0,1:T(8,128)S(1)} %get-tuple-element.3), channel_id=1, replica_groups=mesh['rows'=32,'cols'=4] {'cols'}, dimensions={1}, use_global_device_ids=true | all-gather | bytes 20480 | tf_op jit(solution)/shard_map/all_gather | solution.py:60
  505.1 0.1 copy.122
  505.2 5.8 %cholesky.17 = f32[64,64]{1,0:T(8,128)S(1)} custom-call(f32[64,64]{1,0:T(8,128)S(1)} %fusion.202), custom_call_target="Cholesky" | custom-call | tf_op jit(solution)/shard_map/jit(cholesky)/cholesky | solution.py:65
  511.1 0.6 compare_reduce_fusion
  511.7 0.7 fusion.199
  512.4 4.9 custom-call.6
  517.3 0.2 fusion.200
  517.5 11.9 %all_gather.31 = f32[64,64]{0,1:T(8,128)S(1)} all-gather(f32[64,16]{0,1:T(8,128)S(1)} %get-tuple-element.4), channel_id=1, replica_groups=mesh['rows'=32,'cols'=4] {'cols'}, dimensions={1}, use_global_device_ids=true | all-gather | bytes 20480 | tf_op jit(solution)/shard_map/all_gather | solution.py:64
  529.4 0.2 fusion.203
  529.6 0.2 fusion.241
  529.8 0.6 constant_dynamic-slice_fusion
  530.4 1.9 fusion.206
  (55 shorter events, 1.0 us)
Async XLA Ops:
  7.2 59.2 %all-gather.7.cloned.1.call-start = ((), (), s32[]{:S(2)}) async-start(), calls=%async_computation | async-start | bytes 8650752 | tf_op jit(solution)/shard_map/all_gather | solution.py:42
  9.0 118.3 %all-gather.9.cloned.1.call-start = ((), (), s32[]{:S(2)}) async-start(), calls=%async_computation.1 | async-start | bytes 8650752 | tf_op jit(solution)/shard_map/all_gather | solution.py:42
  9.8 10.1 %collective-permute-start = (bf16[16,1,256]{2,0,1:T(8,128)(2,1)S(1)}, bf16[16,1,256]{2,0,1:T(8,128)(2,1)S(1)}, u32[]{:S(2)}, u32[]{:S(2)}) collective-permute-start(bf16[16,1,256]{2,0,1:T(8,128)(2,1)S(1)} %get-tuple-element.24), channel_id=1, source_target_pairs={{0,4},{4,8},{8,12},{12,16},{16,20},{20,24},{24,28},{28,32},{32,36}... | collective-permute-start | bytes 24584 | tf_op jit(solution)/shard_map/ppermute | solution.py:15
  9.8 13.7 %collective-permute-start.1 = (bf16[16,1,256]{2,0,1:T(8,128)(2,1)S(1)}, bf16[16,1,256]{2,0,1:T(8,128)(2,1)S(1)}, u32[]{:S(2)}, u32[]{:S(2)}) collective-permute-start(bf16[16,1,256]{2,0,1:T(8,128)(2,1)S(1)} %get-tuple-element.23), channel_id=1, source_target_pairs={{4,0},{8,4},{12,8},{16,12},{20,16},{24,20},{28,24},{32,28},{36,32}... | collective-permute-start | bytes 24584 | tf_op jit(solution)/shard_map/ppermute | solution.py:18
  19.9 3.6 copy-start.4
  23.5 50.3 %copy-start.2 = (f32[16,8192]{1,0:T(8,128)S(1)}, f32[16,8192]{1,0:T(8,128)}, u32[]{:S(2)}) copy-start(f32[16,8192]{1,0:T(8,128)} %param.5) | copy-start | bytes 1572868
  74.6 117.0 %all-gather.11.cloned.1.call-start = ((), (), s32[]{:S(2)}) async-start(), calls=%async_computation.2 | async-start | bytes 8650752 | tf_op jit(solution)/shard_map/all_gather | solution.py:42
  75.4 6.2 %collective-permute-start.3 = (bf16[16,1,256]{2,0,1:T(8,128)(2,1)S(1)}, bf16[16,1,256]{2,0,1:T(8,128)(2,1)S(1)}, u32[]{:S(2)}, u32[]{:S(2)}) collective-permute-start(bf16[16,1,256]{2,0,1:T(8,128)(2,1)S(1)} %get-tuple-element.22), channel_id=1, source_target_pairs={{4,0},{8,4},{12,8},{16,12},{20,16},{24,20},{28,24},{32,28},{36,32}... | collective-permute-start | bytes 24584 | tf_op jit(solution)/shard_map/ppermute | solution.py:18
  81.6 53.1 %copy-start.5 = (bf16[2,32,8,256]{3,2,0,1:T(8,128)(2,1)S(1)}, bf16[2,32,8,256]{3,2,0,1:T(8,128)(2,1)}, u32[]{:S(2)}) copy-start(bf16[2,32,8,256]{3,2,0,1:T(8,128)(2,1)} %copy.157) | copy-start | bytes 786436
  81.6 53.1 %collective-permute-start.2 = (bf16[16,1,256]{2,0,1:T(8,128)(2,1)S(1)}, bf16[16,1,256]{2,0,1:T(8,128)(2,1)S(1)}, u32[]{:S(2)}, u32[]{:S(2)}) collective-permute-start(bf16[16,1,256]{2,0,1:T(8,128)(2,1)S(1)} %get-tuple-element.21), channel_id=1, source_target_pairs={{0,4},{4,8},{8,12},{12,16},{16,20},{20,24},{24,28},{28,32},{32,36}... | collective-permute-start | bytes 24584 | tf_op jit(solution)/shard_map/ppermute | solution.py:15
  138.9 117.0 %all-gather.13.cloned.1.call-start = ((), (), s32[]{:S(2)}) async-start(), calls=%async_computation.3 | async-start | bytes 8650752 | tf_op jit(solution)/shard_map/all_gather | solution.py:42
  139.7 6.2 %collective-permute-start.5 = (bf16[16,1,256]{2,0,1:T(8,128)(2,1)S(1)}, bf16[16,1,256]{2,0,1:T(8,128)(2,1)S(1)}, u32[]{:S(2)}, u32[]{:S(2)}) collective-permute-start(bf16[16,1,256]{2,0,1:T(8,128)(2,1)S(1)} %get-tuple-element.20), channel_id=1, source_target_pairs={{4,0},{8,4},{12,8},{16,12},{20,16},{24,20},{28,24},{32,28},{36,32}... | collective-permute-start | bytes 24584 | tf_op jit(solution)/shard_map/ppermute | solution.py:18
  145.9 53.1 %copy-start.6 = (bf16[2,32,8,256]{3,2,0,1:T(8,128)(2,1)S(1)}, bf16[2,32,8,256]{3,2,0,1:T(8,128)(2,1)}, u32[]{:S(2)}) copy-start(bf16[2,32,8,256]{3,2,0,1:T(8,128)(2,1)} %copy.156) | copy-start | bytes 786436
  145.9 53.1 %collective-permute-start.4 = (bf16[16,1,256]{2,0,1:T(8,128)(2,1)S(1)}, bf16[16,1,256]{2,0,1:T(8,128)(2,1)S(1)}, u32[]{:S(2)}, u32[]{:S(2)}) collective-permute-start(bf16[16,1,256]{2,0,1:T(8,128)(2,1)S(1)} %get-tuple-element.19), channel_id=1, source_target_pairs={{0,4},{4,8},{8,12},{12,16},{16,20},{20,24},{24,28},{28,32},{32,36}... | collective-permute-start | bytes 24584 | tf_op jit(solution)/shard_map/ppermute | solution.py:15
  203.3 94.9 %all-gather.15.cloned.1.call-start = ((), (), s32[]{:S(2)}) async-start(), calls=%async_computation.4 | async-start | bytes 2621440 | tf_op jit(solution)/shard_map/all_gather | solution.py:55
  204.0 6.2 %collective-permute-start.7 = (bf16[16,1,256]{2,0,1:T(8,128)(2,1)S(1)}, bf16[16,1,256]{2,0,1:T(8,128)(2,1)S(1)}, u32[]{:S(2)}, u32[]{:S(2)}) collective-permute-start(bf16[16,1,256]{2,0,1:T(8,128)(2,1)S(1)} %get-tuple-element.18), channel_id=1, source_target_pairs={{4,0},{8,4},{12,8},{16,12},{20,16},{24,20},{28,24},{32,28},{36,32}... | collective-permute-start | bytes 24584 | tf_op jit(solution)/shard_map/ppermute | solution.py:18
  210.3 53.1 %copy-start.7 = (bf16[2,32,8,256]{3,2,0,1:T(8,128)(2,1)S(1)}, bf16[2,32,8,256]{3,2,0,1:T(8,128)(2,1)}, u32[]{:S(2)}) copy-start(bf16[2,32,8,256]{3,2,0,1:T(8,128)(2,1)} %copy.155) | copy-start | bytes 786436
  210.3 53.1 %collective-permute-start.6 = (bf16[16,1,256]{2,0,1:T(8,128)(2,1)S(1)}, bf16[16,1,256]{2,0,1:T(8,128)(2,1)S(1)}, u32[]{:S(2)}, u32[]{:S(2)}) collective-permute-start(bf16[16,1,256]{2,0,1:T(8,128)(2,1)S(1)} %get-tuple-element.17), channel_id=1, source_target_pairs={{0,4},{4,8},{8,12},{12,16},{16,20},{20,24},{24,28},{28,32},{32,36}... | collective-permute-start | bytes 24584 | tf_op jit(solution)/shard_map/ppermute | solution.py:15
  267.7 85.7 %all-gather.17.cloned.1.call-start = ((), (), s32[]{:S(2)}) async-start(), calls=%async_computation.5 | async-start | bytes 8650752 | tf_op jit(solution)/shard_map/all_gather | solution.py:42
  269.2 6.2 %collective-permute-start.9 = (bf16[16,1,256]{2,0,1:T(8,128)(2,1)S(1)}, bf16[16,1,256]{2,0,1:T(8,128)(2,1)S(1)}, u32[]{:S(2)}, u32[]{:S(2)}) collective-permute-start(bf16[16,1,256]{2,0,1:T(8,128)(2,1)S(1)} %get-tuple-element.16), channel_id=1, source_target_pairs={{4,0},{8,4},{12,8},{16,12},{20,16},{24,20},{28,24},{32,28},{36,32}... | collective-permute-start | bytes 24584 | tf_op jit(solution)/shard_map/ppermute | solution.py:18
  275.4 22.7 %copy-start.1 = (f32[16,8192]{1,0:T(8,128)S(1)}, f32[16,8192]{1,0:T(8,128)}, u32[]{:S(2)}) copy-start(f32[16,8192]{1,0:T(8,128)} %get-tuple-element.6) | copy-start | bytes 1572868
  275.4 85.3 %copy-start.3 = (bf16[2,32,8,256]{3,2,0,1:T(8,128)(2,1)S(1)}, bf16[2,32,8,256]{3,2,0,1:T(8,128)(2,1)}, u32[]{:S(2)}) copy-start(bf16[2,32,8,256]{3,2,0,1:T(8,128)(2,1)} %copy.154) | copy-start | bytes 786436
  275.4 85.3 %collective-permute-start.8 = (bf16[16,1,256]{2,0,1:T(8,128)(2,1)S(1)}, bf16[16,1,256]{2,0,1:T(8,128)(2,1)S(1)}, u32[]{:S(2)}, u32[]{:S(2)}) collective-permute-start(bf16[16,1,256]{2,0,1:T(8,128)(2,1)S(1)} %get-tuple-element.15), channel_id=1, source_target_pairs={{0,4},{4,8},{8,12},{12,16},{16,20},{20,24},{24,28},{28,32},{32,36}... | collective-permute-start | bytes 24584 | tf_op jit(solution)/shard_map/ppermute | solution.py:15
  360.7 3.6 copy-start
Sparse Core Ops, SparseCore 0:
  10.8 55.4 all-gather.6
  74.7 52.5 all-gather.8
  139.1 52.5 all-gather.10
  203.4 52.5 all-gather.12
  267.8 30.2 all-gather.14
  300.2 53.0 all-gather.16
where the time goes:
time: 540 us; the launch traced here: 539 us
  waiting for transfers between devices  236 us (44%)
  blocking collectives  151 us (28%)
  matrix products  77.1 us (14%)
  local copies, waits for them, and re-layouts  27.9 us (5%)
  starting transfers between devices  17.6 us (3%)
  other arithmetic  14.9 us (3%)
  between operations  14.4 us (3%)
    all_gather x5, waiting for transfers between devices, apply_generator(): piece = lax.all_gather(shaped, 'rows', axis=1, tiled=True)  217 us
    psum x1, blocking collectives, body(): gram_mine = lax.psum(gram_part, 'rows')  127 us
    dot_general x20, matrix products, block_product(): jnp.einsum('jbt,bst->jbs', pieces, blocks[:, position], preferred_element...  69.5 us
    gather x5, local copies, waits for them, and re-layouts, apply_generator(): taken = jnp.take(piece, jnp.clip(far_cols, 0, piece.shape[1] - 1), axis=1)  19.7 us
    all_gather x1, waiting for transfers between devices, body(): whole_iterate = lax.all_gather(iterate, 'cols', axis=0, tiled=True)  18.8 us
    ppermute x5, starting transfers between devices, with_halo(): lax.ppermute(lax.slice_in_dim(block, 0, width, axis=dim), axis, backward)  17.3 us
    all_gather x1, blocking collectives, body(): gram = lax.all_gather(gram_mine, 'cols', axis=1, tiled=True) / total_states  12.4 us
    all_gather x1, blocking collectives, body(): lax.all_gather(product_mine, 'cols', axis=1, tiled=True) / total_states  11.9 us
  transfers between devices with their start and end apart: 16, of which 6 were waited for; matrix products, arithmetic and copies ran while one was open for 14% of the time, Pallas kernels for 0%

commit v1 on v0

--- a/solution.py
+++ b/solution.py
@@ -56,7 +56,7 @@
     contract = (((1,), (1,)), ((), ()))
     gram_part = lax.dot_general(whole_iterate, iterate, contract, precision=highest)
     column_start = lax.axis_index("cols") * width
-    gram_mine = lax.psum(gram_part, "rows")
+    gram_mine = jnp.sum(lax.all_gather(gram_part, "rows"), axis=0)
     gram = lax.all_gather(gram_mine, "cols", axis=1, tiled=True) / total_states
     applied = apply_generator(iterate.astype(jnp.bfloat16))
     product_part = lax.dot_general(whole_iterate, applied, contract, precision=highest)

time: 540 us -> 454 us (0.84)
  waiting for transfers between devices: 236 us -> 184 us
  blocking collectives: 151 us -> 115 us
    psum x1, blocking collectives: 127 us -> 65.3 us  [body(): product_mine = lax.psum(product_part, 'rows')]
    all_gather x5, waiting for transfers between devices: 217 us -> 166 us  [apply_generator(): piece = lax.all_gather(shaped, 'rows', axis=1, tiled=True)]
    all_gather x0 -> x1, blocking collectives: none -> 25 us  [body(): gram_mine = jnp.sum(lax.all_gather(gram_part, 'rows'), axis=0)]
  transfers between devices with their start and end apart: 16 -> 16, of which waited for: 6 -> 5; matrix products, arithmetic and copies ran while one was open for 14% -> 20% of each run, Pallas kernels for 0% -> 0%
where the time goes in v1:
time: 454 us; the launch traced here: 453 us
  waiting for transfers between devices  184 us (41%)
  blocking collectives  115 us (25%)
  matrix products  78.7 us (17%)
  local copies, waits for them, and re-layouts  27.9 us (6%)
  starting transfers between devices  17.5 us (4%)
  other arithmetic  14.9 us (3%)
  between operations  14.5 us (3%)
    all_gather x5, waiting for transfers between devices, apply_generator(): piece = lax.all_gather(shaped, 'rows', axis=1, tiled=True)  166 us
    dot_general x20, matrix products, block_product(): jnp.einsum('jbt,bst->jbs', pieces, blocks[:, position], preferred_element...  69.5 us
    psum x1, blocking collectives, body(): product_mine = lax.psum(product_part, 'rows')  65.3 us
    all_gather x1, blocking collectives, body(): gram_mine = jnp.sum(lax.all_gather(gram_part, 'rows'), axis=0)  25 us
    gather x5, local copies, waits for them, and re-layouts, apply_generator(): taken = jnp.take(piece, jnp.clip(far_cols, 0, piece.shape[1] - 1), axis=1)  19.7 us
    all_gather x1, waiting for transfers between devices, body(): whole_iterate = lax.all_gather(iterate, 'cols', axis=0, tiled=True)  18.9 us
    ppermute x5, starting transfers between devices, with_halo(): lax.ppermute(lax.slice_in_dim(block, 0, width, axis=dim), axis, backward)  17.3 us
    all_gather x1, blocking collectives, body(): lax.all_gather(product_mine, 'cols', axis=1, tiled=True) / total_states  12.2 us
  transfers between devices with their start and end apart: 16, of which 5 were waited for; matrix products, arithmetic and copies ran while one was open for 20% of the time, Pallas kernels for 0%

profile of v1, /device:TPU:0, one launch (start us, length us, event | category | flops | bytes accessed | tf_op | source)
XLA Modules:
  0.0 452.6 jit_solution(6914848809600684148)
XLA Ops:
  7.2 1.1 convert_element_type.16
  8.3 0.7 copy.158
  9.1 0.7 fusion.238
  9.8 6.0 %collective-permute-start.1 = (bf16[16,1,256]{2,0,1:T(8,128)(2,1)S(1)}, bf16[16,1,256]{2,0,1:T(8,128)(2,1)S(1)}, u32[]{:S(2)}, u32[]{:S(2)}) collective-permute-start(bf16[16,1,256]{2,0,1:T(8,128)(2,1)S(1)} %get-tuple-element.21), channel_id=1, source_target_pairs={{4,0},{8,4},{12,8},{16,12},{20,16},{24,20},{28,24},{32,28},{36,32}... | collective-permute-start | bytes 24584 | tf_op jit(solution)/shard_map/ppermute | solution.py:18
  15.8 0.7 compare_and_fusion
  16.5 3.4 fusion.60
  19.9 3.6 fusion.84
  23.5 3.5 fusion.81
  27.0 39.3 %all-gather.9.cloned.1.call-done = bf16[16,1024,256]{2,0,1:T(8,128)(2,1)} async-done(((bf16[16,32,256]{2,0,1:T(8,128)(2,1)}), bf16[16,1024,256]{2,0,1:T(8,128)(2,1)}) %all-gather.9.cloned.1.call-update) | async-done | bytes 8388624 | tf_op jit(solution)/shard_map/all_gather | solution.py:42
  66.4 3.9 gather_fusion
  70.3 3.4 fusion.72
  73.9 0.7 copy.157
  74.7 0.7 fusion.237
  75.4 2.8 collective-permute-start.3
  78.2 3.4 fusion.36
  81.6 3.6 fusion.16
  85.2 42.1 %all-gather.11.cloned.1.call-done = bf16[16,1024,256]{2,0,1:T(8,128)(2,1)} async-done(((bf16[16,32,256]{2,0,1:T(8,128)(2,1)}), bf16[16,1024,256]{2,0,1:T(8,128)(2,1)}) %all-gather.11.cloned.1.call-update) | async-done | bytes 8388624 | tf_op jit(solution)/shard_map/all_gather | solution.py:42
  127.3 3.9 gather_fusion.1
  131.2 3.4 fusion.6
  134.7 3.4 fusion.141
  138.2 0.7 copy.156
  139.0 0.7 fusion.236
  139.7 2.8 collective-permute-start.5
  142.5 3.4 fusion.34
  145.9 3.6 fusion.14
  149.6 42.1 %all-gather.13.cloned.1.call-done = bf16[16,1024,256]{2,0,1:T(8,128)(2,1)} async-done(((bf16[16,32,256]{2,0,1:T(8,128)(2,1)}), bf16[16,1024,256]{2,0,1:T(8,128)(2,1)}) %all-gather.13.cloned.1.call-update) | async-done | bytes 8388624 | tf_op jit(solution)/shard_map/all_gather | solution.py:42
  191.6 3.9 gather_fusion.2
  195.6 3.4 fusion.4
  199.0 3.4 fusion.129
  202.5 0.7 copy.155
  203.3 0.7 fusion.235
  204.0 2.8 collective-permute-start.7
  206.9 3.4 fusion.32
  210.3 3.6 fusion.12
  213.9 42.1 %all-gather.15.cloned.1.call-done = bf16[16,1024,256]{2,0,1:T(8,128)(2,1)} async-done(((bf16[16,32,256]{2,0,1:T(8,128)(2,1)}), bf16[16,1024,256]{2,0,1:T(8,128)(2,1)}) %all-gather.15.cloned.1.call-update) | async-done | bytes 8388624 | tf_op jit(solution)/shard_map/all_gather | solution.py:42
  256.0 3.9 gather_fusion.3
  259.9 3.4 fusion.2
  263.3 3.4 fusion.117
  266.8 0.9 fusion.230
  267.7 0.7 copy.154
  268.5 0.7 fusion.234
  269.2 2.8 collective-permute-start.9
  272.0 3.4 fusion.30
  275.4 3.8 fusion.10
  279.3 18.9 %all-gather.17.cloned.1.call-done = f32[64,8192]{1,0:T(8,128)} async-done(((f32[16,8192]{1,0:T(8,128)}), f32[64,8192]{1,0:T(8,128)}) %all-gather.17.cloned.1.call-update) | async-done | bytes 2097168 | tf_op jit(solution)/shard_map/all_gather | solution.py:55
  298.1 3.3 convolution_bitcast_fusion
  301.5 25.0 %all-gather.1 = f32[32,64,16]{1,2,0:T(8,128)S(1)} all-gather(f32[1,64,16]{1,2,0:T(8,128)S(1)} %convolution_bitcast_fusion), channel_id=2, replica_groups=mesh['rows'=32,'cols'=4] {'rows'}, dimensions={0}, use_global_device_ids=true | all-gather | bytes 135168 | tf_op jit(solution)/shard_map/all_gather | solution.py:59
  326.5 12.1 %all_gather.37 = f32[64,64]{0,1:T(8,128)S(1)} all-gather(f32[64,16]{0,1:T(8,128)S(1)} %reduce_sum.9), channel_id=1, replica_groups=mesh['rows'=32,'cols'=4] {'cols'}, dimensions={1}, use_global_device_ids=true | all-gather | bytes 20480 | tf_op jit(solution)/shard_map/all_gather | solution.py:60
  338.6 0.1 copy.122
  338.7 5.8 %cholesky.17 = f32[64,64]{1,0:T(8,128)S(1)} custom-call(f32[64,64]{1,0:T(8,128)S(1)} %fusion.202), custom_call_target="Cholesky" | custom-call | tf_op jit(solution)/shard_map/jit(cholesky)/cholesky | solution.py:65
  344.6 0.6 compare_reduce_fusion
  345.3 0.7 fusion.199
  345.9 4.9 %custom-call.6 = f32[1,64,64]{1,2,0:T(8,128)S(1)} custom-call(f32[1,64,64]{2,1,0:T(8,128)S(1)} %fusion.199), custom_call_target="InvertDiagBlocksLowerTriangular" | custom-call | tf_op jit(solution)/shard_map/triangular_solve | solution.py:67
  350.8 0.2 fusion.200
  351.1 3.5 fusion.206
  354.6 3.9 gather_fusion.4
  358.5 3.4 fusion
  361.9 3.5 fusion.105
  365.5 1.7 fusion.239
  367.3 65.3 %psum.7 = f32[64,16]{0,1:T(8,128)S(1)} all-reduce(f32[64,16]{0,1:T(8,128)S(1)} %fusion.239), channel_id=1, replica_groups=mesh['rows'=32,'cols'=4] {'rows'}, use_global_device_ids=true, to_apply=%region_3.5 | all-reduce | flops 1024 | bytes 8192 | tf_op jit(solution)/shard_map/psum | solution.py:63
  432.6 12.2 %all_gather.39 = f32[64,64]{0,1:T(8,128)S(1)} all-gather(f32[64,16]{0,1:T(8,128)S(1)} %psum.7), channel_id=1, replica_groups=mesh['rows'=32,'cols'=4] {'cols'}, dimensions={1}, use_global_device_ids=true | all-gather | bytes 20480 | tf_op jit(solution)/shard_map/all_gather | solution.py:64
  444.8 0.2 fusion.203
  445.0 0.2 fusion.240
  445.2 0.6 constant_dynamic-slice_fusion
  (57 shorter events, 1.0 us)
Async XLA Ops:
  7.2 59.2 %all-gather.9.cloned.1.call-start = ((), (), s32[]{:S(2)}) async-start(), calls=%async_computation | async-start | bytes 8650752 | tf_op jit(solution)/shard_map/all_gather | solution.py:42
  9.0 118.3 %all-gather.11.cloned.1.call-start = ((), (), s32[]{:S(2)}) async-start(), calls=%async_computation.1 | async-start | bytes 8650752 | tf_op jit(solution)/shard_map/all_gather | solution.py:42
  9.8 10.1 %collective-permute-start = (bf16[16,1,256]{2,0,1:T(8,128)(2,1)S(1)}, bf16[16,1,256]{2,0,1:T(8,128)(2,1)S(1)}, u32[]{:S(2)}, u32[]{:S(2)}) collective-permute-start(bf16[16,1,256]{2,0,1:T(8,128)(2,1)S(1)} %get-tuple-element.22), channel_id=1, source_target_pairs={{0,4},{4,8},{8,12},{12,16},{16,20},{20,24},{24,28},{28,32},{32,36}... | collective-permute-start | bytes 24584 | tf_op jit(solution)/shard_map/ppermute | solution.py:15
  9.8 13.7 %collective-permute-start.1 = (bf16[16,1,256]{2,0,1:T(8,128)(2,1)S(1)}, bf16[16,1,256]{2,0,1:T(8,128)(2,1)S(1)}, u32[]{:S(2)}, u32[]{:S(2)}) collective-permute-start(bf16[16,1,256]{2,0,1:T(8,128)(2,1)S(1)} %get-tuple-element.21), channel_id=1, source_target_pairs={{4,0},{8,4},{12,8},{16,12},{20,16},{24,20},{28,24},{32,28},{36,32}... | collective-permute-start | bytes 24584 | tf_op jit(solution)/shard_map/ppermute | solution.py:18
  19.9 3.6 copy-start.4
  23.5 50.3 %copy-start.2 = (f32[16,8192]{1,0:T(8,128)S(1)}, f32[16,8192]{1,0:T(8,128)}, u32[]{:S(2)}) copy-start(f32[16,8192]{1,0:T(8,128)} %param.5) | copy-start | bytes 1572868
  74.6 117.0 %all-gather.13.cloned.1.call-start = ((), (), s32[]{:S(2)}) async-start(), calls=%async_computation.2 | async-start | bytes 8650752 | tf_op jit(solution)/shard_map/all_gather | solution.py:42
  75.4 6.2 %collective-permute-start.3 = (bf16[16,1,256]{2,0,1:T(8,128)(2,1)S(1)}, bf16[16,1,256]{2,0,1:T(8,128)(2,1)S(1)}, u32[]{:S(2)}, u32[]{:S(2)}) collective-permute-start(bf16[16,1,256]{2,0,1:T(8,128)(2,1)S(1)} %get-tuple-element.20), channel_id=1, source_target_pairs={{4,0},{8,4},{12,8},{16,12},{20,16},{24,20},{28,24},{32,28},{36,32}... | collective-permute-start | bytes 24584 | tf_op jit(solution)/shard_map/ppermute | solution.py:18
  81.6 53.1 %copy-start.5 = (bf16[2,32,8,256]{3,2,0,1:T(8,128)(2,1)S(1)}, bf16[2,32,8,256]{3,2,0,1:T(8,128)(2,1)}, u32[]{:S(2)}) copy-start(bf16[2,32,8,256]{3,2,0,1:T(8,128)(2,1)} %copy.157) | copy-start | bytes 786436
  81.6 53.1 %collective-permute-start.2 = (bf16[16,1,256]{2,0,1:T(8,128)(2,1)S(1)}, bf16[16,1,256]{2,0,1:T(8,128)(2,1)S(1)}, u32[]{:S(2)}, u32[]{:S(2)}) collective-permute-start(bf16[16,1,256]{2,0,1:T(8,128)(2,1)S(1)} %get-tuple-element.19), channel_id=1, source_target_pairs={{0,4},{4,8},{8,12},{12,16},{16,20},{20,24},{24,28},{28,32},{32,36}... | collective-permute-start | bytes 24584 | tf_op jit(solution)/shard_map/ppermute | solution.py:15
  138.9 117.0 %all-gather.15.cloned.1.call-start = ((), (), s32[]{:S(2)}) async-start(), calls=%async_computation.3 | async-start | bytes 8650752 | tf_op jit(solution)/shard_map/all_gather | solution.py:42
  139.7 6.2 %collective-permute-start.5 = (bf16[16,1,256]{2,0,1:T(8,128)(2,1)S(1)}, bf16[16,1,256]{2,0,1:T(8,128)(2,1)S(1)}, u32[]{:S(2)}, u32[]{:S(2)}) collective-permute-start(bf16[16,1,256]{2,0,1:T(8,128)(2,1)S(1)} %get-tuple-element.18), channel_id=1, source_target_pairs={{4,0},{8,4},{12,8},{16,12},{20,16},{24,20},{28,24},{32,28},{36,32}... | collective-permute-start | bytes 24584 | tf_op jit(solution)/shard_map/ppermute | solution.py:18
  145.9 53.1 %copy-start.6 = (bf16[2,32,8,256]{3,2,0,1:T(8,128)(2,1)S(1)}, bf16[2,32,8,256]{3,2,0,1:T(8,128)(2,1)}, u32[]{:S(2)}) copy-start(bf16[2,32,8,256]{3,2,0,1:T(8,128)(2,1)} %copy.156) | copy-start | bytes 786436
  145.9 53.1 %collective-permute-start.4 = (bf16[16,1,256]{2,0,1:T(8,128)(2,1)S(1)}, bf16[16,1,256]{2,0,1:T(8,128)(2,1)S(1)}, u32[]{:S(2)}, u32[]{:S(2)}) collective-permute-start(bf16[16,1,256]{2,0,1:T(8,128)(2,1)S(1)} %get-tuple-element.17), channel_id=1, source_target_pairs={{0,4},{4,8},{8,12},{12,16},{16,20},{20,24},{24,28},{28,32},{32,36}... | collective-permute-start | bytes 24584 | tf_op jit(solution)/shard_map/ppermute | solution.py:15
  203.3 94.9 %all-gather.17.cloned.1.call-start = ((), (), s32[]{:S(2)}) async-start(), calls=%async_computation.4 | async-start | bytes 2621440 | tf_op jit(solution)/shard_map/all_gather | solution.py:55
  204.0 6.2 %collective-permute-start.7 = (bf16[16,1,256]{2,0,1:T(8,128)(2,1)S(1)}, bf16[16,1,256]{2,0,1:T(8,128)(2,1)S(1)}, u32[]{:S(2)}, u32[]{:S(2)}) collective-permute-start(bf16[16,1,256]{2,0,1:T(8,128)(2,1)S(1)} %get-tuple-element.16), channel_id=1, source_target_pairs={{4,0},{8,4},{12,8},{16,12},{20,16},{24,20},{28,24},{32,28},{36,32}... | collective-permute-start | bytes 24584 | tf_op jit(solution)/shard_map/ppermute | solution.py:18
  210.3 53.1 %copy-start.7 = (bf16[2,32,8,256]{3,2,0,1:T(8,128)(2,1)S(1)}, bf16[2,32,8,256]{3,2,0,1:T(8,128)(2,1)}, u32[]{:S(2)}) copy-start(bf16[2,32,8,256]{3,2,0,1:T(8,128)(2,1)} %copy.155) | copy-start | bytes 786436
  210.3 53.1 %collective-permute-start.6 = (bf16[16,1,256]{2,0,1:T(8,128)(2,1)S(1)}, bf16[16,1,256]{2,0,1:T(8,128)(2,1)S(1)}, u32[]{:S(2)}, u32[]{:S(2)}) collective-permute-start(bf16[16,1,256]{2,0,1:T(8,128)(2,1)S(1)} %get-tuple-element.15), channel_id=1, source_target_pairs={{0,4},{4,8},{8,12},{12,16},{16,20},{20,24},{24,28},{28,32},{32,36}... | collective-permute-start | bytes 24584 | tf_op jit(solution)/shard_map/ppermute | solution.py:15
  267.7 86.9 %all-gather.19.cloned.1.call-start = ((), (), s32[]{:S(2)}) async-start(), calls=%async_computation.5 | async-start | bytes 8650752 | tf_op jit(solution)/shard_map/all_gather | solution.py:42
  269.2 6.2 %collective-permute-start.9 = (bf16[16,1,256]{2,0,1:T(8,128)(2,1)S(1)}, bf16[16,1,256]{2,0,1:T(8,128)(2,1)S(1)}, u32[]{:S(2)}, u32[]{:S(2)}) collective-permute-start(bf16[16,1,256]{2,0,1:T(8,128)(2,1)S(1)} %get-tuple-element.14), channel_id=1, source_target_pairs={{4,0},{8,4},{12,8},{16,12},{20,16},{24,20},{28,24},{32,28},{36,32}... | collective-permute-start | bytes 24584 | tf_op jit(solution)/shard_map/ppermute | solution.py:18
  275.4 22.7 %copy-start.1 = (f32[16,8192]{1,0:T(8,128)S(1)}, f32[16,8192]{1,0:T(8,128)}, u32[]{:S(2)}) copy-start(f32[16,8192]{1,0:T(8,128)} %get-tuple-element.4) | copy-start | bytes 1572868
  275.4 86.5 %collective-permute-start.8 = (bf16[16,1,256]{2,0,1:T(8,128)(2,1)S(1)}, bf16[16,1,256]{2,0,1:T(8,128)(2,1)S(1)}, u32[]{:S(2)}, u32[]{:S(2)}) collective-permute-start(bf16[16,1,256]{2,0,1:T(8,128)(2,1)S(1)} %get-tuple-element.13), channel_id=1, source_target_pairs={{0,4},{4,8},{8,12},{12,16},{16,20},{20,24},{24,28},{28,32},{32,36}... | collective-permute-start | bytes 24584 | tf_op jit(solution)/shard_map/ppermute | solution.py:15
  279.3 82.7 %copy-start.3 = (bf16[2,32,8,256]{3,2,0,1:T(8,128)(2,1)S(1)}, bf16[2,32,8,256]{3,2,0,1:T(8,128)(2,1)}, u32[]{:S(2)}) copy-start(bf16[2,32,8,256]{3,2,0,1:T(8,128)(2,1)} %copy.154) | copy-start | bytes 786436
  361.9 3.6 copy-start
Sparse Core Ops, SparseCore 0:
  10.8 55.4 all-gather.8
  74.7 52.5 all-gather.10
  139.1 52.5 all-gather.12
  203.4 52.5 all-gather.14
  267.8 30.2 all-gather.16
  300.2 53.0 all-gather.18
